TPU v7x, 512 devices: a whole 4x8x8 slice. The times are simulated.
512 devices in a mesh: row: 16 (over z_hi, x), col: 32 (over z_lo, y, core).
Axes of the slice: x: 4, y: 8, z: 8 (z_hi: 4, z_lo: 2; z = z_hi * 2 + z_lo), core: 2. Of those that a mesh axis runs over, the one named last changes fastest.
Arguments:
- samples: bfloat16 [32768, 64], P(('row', 'col')), may hold values from -6 to 6
- scores: bfloat16 [32768, 64], P(('row', 'col')), may hold values from -6 to 6
- tile_groups: int32 [16, 32], P('row', 'col'), may hold values from 1 to 8, as said below
Outputs:
- grad_samples: float32 [32768, 64], P(('row', 'col'))
- grad_scores: float32 [32768, 64], P(('row', 'col'))
- loss: float32 [], replicated
Inputs may be any that keep to these rules, and one draw needn't show every extreme that they name: `tile_groups`: the number of column groups of 128 samples that each tile uses, counted from the start of its column block; the value 8 occurs in every draw.
All inputs are finite; a program needn't handle non-finite values.
Results may differ from a plain program's by a relative error of at most 0.0011.
Values may be sent and summed in bfloat16 or wider, within the bound.
A program may use at most 64 MiB of HBM per device.

v0:
```python
import jax
import jax.numpy as jnp
from jax import lax
from jax.sharding import PartitionSpec as P

SPAN = 128


def tile_terms(rows, cols, active, row_index, col_index, m_dev, offset):
    width = rows.shape[1] // 2
    h_two = float(width)
    x_rows = rows[:, :width]
    s_rows = rows[:, width:]
    x_cols = cols[:, :width]
    s_cols = cols[:, width:]
    g_xx = jnp.dot(x_rows, x_cols.T, preferred_element_type=jnp.float32)
    g_xs = jnp.dot(x_rows, s_cols.T, preferred_element_type=jnp.float32)
    g_sx = jnp.dot(s_rows, x_cols.T, preferred_element_type=jnp.float32)
    g_ss = jnp.dot(s_rows, s_cols.T, preferred_element_type=jnp.float32)
    xr32 = x_rows.astype(jnp.float32)
    sr32 = s_rows.astype(jnp.float32)
    xc32 = x_cols.astype(jnp.float32)
    sc32 = s_cols.astype(jnp.float32)
    norm_rows = jnp.sum(xr32 * xr32, axis=1)
    norm_cols = jnp.sum(xc32 * xc32, axis=1)
    self_rows = jnp.sum(xr32 * sr32, axis=1)
    self_cols = jnp.sum(xc32 * sc32, axis=1)
    dist = norm_rows[:, None] + norm_cols[None, :] - 2.0 * g_xx
    kernel = jnp.exp(-dist / (2.0 * h_two))
    stein = (
        g_ss
        + (self_rows[:, None] - g_sx - g_xs + self_cols[None, :]) / h_two
        + width / h_two
        - dist / (h_two * h_two)
    )
    row_pos = jnp.arange(rows.shape[0], dtype=jnp.int32)[:, None]
    col_pos = jnp.arange(cols.shape[0], dtype=jnp.int32)[None, :] + offset
    local_row = row_pos - col_index * m_dev
    local_col = col_pos - row_index * m_dev
    diagonal = (local_row == local_col) & (local_row >= 0) & (local_row < m_dev)
    keep = (col_pos // SPAN < active) & jnp.logical_not(diagonal)
    kept = jnp.where(keep, kernel, jnp.float32(0.0))
    loss = jnp.sum(kept * stein)
    count = jnp.sum(keep.astype(jnp.float32))
    coef = kept * (stein / h_two + 2.0 / (h_two * h_two))
    kept_half = kept.astype(jnp.bfloat16)
    coef_half = coef.astype(jnp.bfloat16)
    ksum_rows = jnp.sum(kept, axis=1)[:, None]
    csum_rows = jnp.sum(coef, axis=1)[:, None]
    ksum_cols = jnp.sum(kept, axis=0)[:, None]
    csum_cols = jnp.sum(coef, axis=0)[:, None]
    k_cols = jnp.dot(kept_half, cols, preferred_element_type=jnp.float32)
    a_cols = jnp.dot(coef_half, x_cols, preferred_element_type=jnp.float32)
    dims = (((0,), (0,)), ((), ()))
    k_rows = lax.dot_general(kept_half, rows, dims, preferred_element_type=jnp.float32)
    a_rows = lax.dot_general(coef_half, x_rows, dims, preferred_element_type=jnp.float32)
    row_gx = a_cols - xr32 * csum_rows + (sr32 * ksum_rows - k_cols[:, width:]) / h_two
    row_gs = k_cols[:, width:] + (xr32 * ksum_rows - k_cols[:, :width]) / h_two
    col_gx = a_rows - xc32 * csum_cols - (k_rows[:, width:] - sc32 * ksum_cols) / h_two
    col_gs = k_rows[:, width:] - (k_rows[:, :width] - xc32 * ksum_cols) / h_two
    row_grad = jnp.concatenate([row_gx, row_gs], axis=1)
    col_grad = jnp.concatenate([col_gx, col_gs], axis=1)
    return (loss, count, row_grad, col_grad)


def shards(samples, scores, tile_groups):
    m_dev = samples.shape[0]
    width = samples.shape[1]
    local_pair = jnp.concatenate([samples, scores], axis=1)
    rows = lax.all_gather(local_pair, "col", axis=0, tiled=True)
    cols = lax.all_gather(local_pair, "row", axis=0, tiled=True)
    row_index = lax.axis_index("row")
    col_index = lax.axis_index("col")
    active = tile_groups[0, 0]
    number = cols.shape[0] // SPAN

    def accumulate(group, carry):
        loss_sum, count_sum, row_acc, col_acc = carry
        start = (group * SPAN).astype(jnp.int32)
        block = lax.dynamic_slice_in_dim(cols, start, SPAN, 0)
        loss, count, row_grad, col_grad = tile_terms(
            rows, block, active, row_index, col_index, m_dev, start
        )
        col_acc = lax.dynamic_update_slice_in_dim(col_acc, col_grad, start, 0)
        return (loss_sum + loss, count_sum + count, row_acc + row_grad, col_acc)

    init = (
        jnp.float32(0.0),
        jnp.float32(0.0),
        jnp.zeros((rows.shape[0], 2 * width), jnp.float32),
        jnp.zeros((cols.shape[0], 2 * width), jnp.float32),
    )
    loss_sum, count_sum, row_acc, col_acc = lax.fori_loop(0, number, accumulate, init)
    row_share = lax.psum_scatter(row_acc, "col", scatter_dimension=0, tiled=True)
    col_share = lax.psum_scatter(col_acc, "row", scatter_dimension=0, tiled=True)
    total, pairs = lax.psum((loss_sum, count_sum), ("row", "col"))
    everyone = float(m_dev * lax.axis_size("row") * lax.axis_size("col"))
    grads = (row_share + col_share) * (everyone / pairs)
    return (grads[:, :width], grads[:, width:], total / pairs)


def solution(mesh):
    placed = (P(("row", "col"), None), P(("row", "col"), None), P("row", "col"))
    return jax.shard_map(
        shards,
        mesh=mesh,
        in_specs=placed,
        out_specs=(P(("row", "col"), None), P(("row", "col"), None), P()),
        check_vma=False,
    )
```

profile of v0, /device:TPU:1, one launch (start us, length us, event | category | flops | bytes accessed | tf_op | source)
XLA Modules:
  0.0 383.4 jit_solution(5438793085541938795)
XLA Ops:
  7.2 0.8 pad_maximum_fusion.1
  8.0 38.5 %all_gather.6 = bf16[2048,128]{1,0:T(8,128)(2,1)S(1)} all-gather(bf16[64,128]{1,0:T(8,128)(2,1)S(1)} %pad_maximum_fusion.1), channel_id=1, replica_groups=mesh['row'=16,'col'=32] {'col'}, dimensions={0}, use_global_device_ids=true | all-gather | bytes 540672 | tf_op jit(solution)/shard_map/all_gather | solution.py:70
  46.5 44.9 %all_gather.7 = bf16[1024,128]{1,0:T(8,128)(2,1)} all-gather(bf16[64,128]{1,0:T(8,128)(2,1)S(1)} %pad_maximum_fusion.1), channel_id=1, replica_groups=mesh['row'=16,'col'=32] {'row'}, dimensions={0}, use_global_device_ids=true | all-gather | bytes 278528 | tf_op jit(solution)/shard_map/all_gather | solution.py:71
  91.7 0.9 broadcast_in_dim.48.clone
  92.5 78.0 %while.22 = (s32[]{:T(128)}, f32[]{:T(128)}, f32[]{:T(128)}, f32[2048,128]{0,1:T(8,128)S(1)}, f32[1024,128]{1,0:T(8,128)}, /*index=5*/s32[]{:T(128)}, s32[]{:T(1...) while((s32[]{:T(128)}, f32[]{:T(128)}, f32[]{:T(128)}, ...), condition=%wide.region_11.12_spmd.clone, body=%wide.region_0.11_spmd.clone.sunk | while | flops 351840128 | bytes 21069464 | solution.py:93
  92.5 0.9 fusion.100
  94.7 0.7 fusion.106
  95.4 1.9 fusion.108
  98.2 0.6 constant_dynamic-update-slice_fusion.2
  98.9 1.4 fusion.109
  102.2 0.9 fusion.100
  104.4 0.7 fusion.106
  105.1 1.9 fusion.108
  108.6 1.4 fusion.109
  112.0 0.9 fusion.100
  114.2 0.7 fusion.106
  114.9 1.9 fusion.108
  117.8 0.6 constant_dynamic-update-slice_fusion.2
  118.4 1.4 fusion.109
  121.7 0.9 fusion.100
  123.9 0.7 fusion.106
  124.6 1.9 fusion.108
  127.5 0.6 constant_dynamic-update-slice_fusion.2
  128.1 1.4 fusion.109
  131.5 0.9 fusion.100
  133.7 0.7 fusion.106
  134.4 1.9 fusion.108
  137.9 1.4 fusion.109
  141.2 0.9 fusion.100
  143.4 0.7 fusion.106
  144.1 1.9 fusion.108
  147.0 0.6 constant_dynamic-update-slice_fusion.2
  147.6 1.4 fusion.109
  151.0 0.9 fusion.100
  153.2 0.7 fusion.106
  153.9 1.9 fusion.108
  156.7 0.6 constant_dynamic-update-slice_fusion.2
  157.4 1.4 fusion.109
  160.7 0.9 fusion.100
  162.9 0.7 fusion.106
  163.6 1.9 fusion.108
  166.5 0.6 constant_dynamic-update-slice_fusion.2
  167.1 1.4 fusion.109
  170.6 1.3 copy.12
  171.9 101.4 %all-reduce = (f32[]{:T(128)}, f32[]{:T(128)}) all-reduce(f32[]{:T(128)} %get-tuple-element.255, f32[]{:T(128)} %get-tuple-element.256), channel_id=1, replica_groups=mesh['row'=16,'col'=32] {'row','col'}, use_global_device_ids=true, to_apply=%region_14.15 | all-reduce | flops 2 | bytes 16 | tf_op jit(solution)/shard_map/psum | solution.py:96
  275.3 98.6 %reduce-scatter.3.cloned.1.call-done = f32[64,128]{1,0:T(8,128)} async-done(((f32[2048,128]{1,0:T(8,128)}), f32[64,128]{1,0:T(8,128)}) %reduce-scatter.3.cloned.1.call-update) | async-done | bytes 32784 | tf_op jit(solution)/shard_map/reduce_scatter | solution.py:94
  373.9 0.8 add_multiply_fusion.1
  374.7 0.7 fusion.46
  (153 shorter events, 24.8 us)
Async XLA Ops:
  7.2 268.2 %reduce-scatter.5.cloned.1.call-start = ((), (), s32[]{:S(2)}) async-start(), calls=%async_computation.3 | async-start | bytes 557056 | tf_op jit(solution)/shard_map/reduce_scatter | solution.py:95
  170.5 203.4 %reduce-scatter.3.cloned.1.call-start = ((), (), s32[]{:S(2)}) async-start(), calls=%async_computation.2 | async-start | bytes 1081344 | tf_op jit(solution)/shard_map/reduce_scatter | solution.py:94
Sparse Core Ops, SparseCore 0:
  170.6 84.6 reduce-scatter.4
  258.3 115.5 reduce-scatter.2
where the time goes:
time: 387 us; the launch traced here: 383 us
  blocking collectives  185 us (48%)
  waiting for transfers between devices  98.6 us (25%)
  matrix products  41.8 us (11%)
  local copies, waits for them, and re-layouts  17.6 us (5%)
  between operations  17.2 us (4%)
  other arithmetic  12.1 us (3%)
  loops' own time  11.2 us (3%)
    psum x1, blocking collectives, shards(): total, pairs = lax.psum((loss_sum, count_sum), ('row', 'col'))  101 us
    reduce_scatter x1, waiting for transfers between devices, shards(): lax.psum_scatter(row_acc, 'col', scatter_dimension=0, tiled=True)  98.6 us
    all_gather x1, blocking collectives, shards(): cols = lax.all_gather(local_pair, 'row', axis=0, tiled=True)  44.9 us
    all_gather x1, blocking collectives, shards(): rows = lax.all_gather(local_pair, 'col', axis=0, tiled=True)  38.5 us
    dot_general x8, matrix products, tile_terms(): g_xs = jnp.dot(x_rows, s_cols.T, preferred_element_type=jnp.float32)  14.9 us
    another operation x1, loops' own time, shards(): lax.fori_loop(0, number, accumulate, init)  11.2 us
    dot_general x8, matrix products, tile_terms(): k_cols = jnp.dot(kept_half, cols, preferred_element_type=jnp.float32)  11 us
    while x24, local copies, waits for them, and re-layouts  8.81 us
  transfers between devices with their start and end apart: 2, of which 1 were waited for; matrix products, arithmetic and copies ran while one was open for 0% of the time, Pallas kernels for 0%

commit v1 on v0

v1 whole, which is shorter than its diff:
```python
import jax
import ml_dtypes
import jax.numpy as jnp
from jax import lax
from jax.experimental import pallas as pl
from jax.experimental.pallas import tpu as pltpu
from jax.sharding import PartitionSpec as P

MESH = pl.DeviceIdType.MESH
F32 = jnp.float32
BF16 = jnp.bfloat16

NROW, NCOL = 16, 32
M = 64
CHUNKS = 9
RG = 2 * CHUNKS
SUPER = 3
RS_GROUPS = RG // SUPER
RROWS = RS_GROUPS * M
QUART = 4
QCOLS = 4 * M
EVERYONE = float(M * NROW * NCOL)
BIG = -16384.0

OFFSETS = (
    (0, 4, True), (0, 3, False), (1, -3, False),
    (1, None, False), (1, 2, False), (0, -2, False),
    (0, 1, False), (1, -1, False), (0, 0, True),
)


def split3(value):
    hi = value.astype(BF16).astype(F32)
    rest = value - hi
    mid = rest.astype(BF16).astype(F32)
    return hi, mid, rest - mid


def dot(a, b):
    return lax.dot_general(a, b, (((1,), (0,)), ((), ())), preferred_element_type=F32)


def dot_nt(a, b):
    return lax.dot_general(a, b, (((1,), (1,)), ((), ())), preferred_element_type=F32)


def lanes(rows=1, width=128):
    return lax.broadcasted_iota(jnp.int32, (rows, width), 1)


def squares(p, sw):
    q = p * jnp.where(lanes() < 64, p, sw)
    hi = q.astype(BF16)
    return jnp.concatenate([hi, (q - hi.astype(F32)).astype(BF16)], axis=1)


def sum_weights(e_lanes, s_lanes):
    k = lax.broadcasted_iota(jnp.int32, (256, 128), 0) % 128
    lane = lax.broadcasted_iota(jnp.int32, (256, 128), 1)
    is_x = k < 64
    out = jnp.zeros((256, 128), F32)
    if e_lanes is not None:
        in_e = (lane >= e_lanes) & (lane < e_lanes + 3)
        out = jnp.where(in_e & is_x, -(2.0 ** -7), out)
    if s_lanes is not None:
        in_s = (lane >= s_lanes) & (lane < s_lanes + 3)
        out = jnp.where(in_s, jnp.where(is_x, -(2.0 ** -18), 2.0 ** -12), out)
    return out.astype(BF16)


def pick3(value):
    hi, mid, lo = split3(value)
    part = lanes() % 3
    return jnp.where(part == 0, hi, jnp.where(part == 1, mid, lo))


def prep_rows(ref, step):
    pair = ref.rowbuf[pl.ds(step * RS_GROUPS, RS_GROUPS)].reshape(RROWS, 128)
    p = pair.astype(F32)
    sw = pltpu.roll(p, 64, 1)
    lane = lanes(RROWS)
    group = lax.broadcasted_iota(jnp.int32, (RROWS, 128), 0) // M + step * RS_GROUPS
    sums = dot(squares(p, sw), sum_weights(0, 6))
    one = ((lane >= 3) & (lane < 6)) | (lane == 9)
    one = one | (lane == 10 + group) | (lane == 10 + RG + group) | (lane == 10 + 2 * RG + group)
    misc = pick3(sums) + one.astype(F32)
    ext = jnp.where(lane < 64, misc, p).astype(BF16)
    ref.a_op[pl.ds(step * RROWS, RROWS), :] = jnp.concatenate([pair, ext], axis=1)
    pt = p.T
    xt, st = pt[0:64], pt[64:128]
    ones = jnp.ones((16, RROWS), F32)
    ref.f1t[step] = jnp.concatenate([st * (-1.0 / 64), st, xt * (-1.0 / 64), ones], axis=0).astype(BF16)
    ref.f2t[step] = jnp.concatenate([xt, ones], axis=0).astype(BF16)


def prep_cols(ref, quarter):
    pair = ref.colbuf[pl.ds(quarter * 4, 4)].reshape(QCOLS, 128)
    p = pair.astype(F32)
    sw = pltpu.roll(p, 64, 1)
    lane = lanes()
    first = lane < 64
    sq = squares(p, sw)
    sums_e = dot(sq, sum_weights(3, None))
    sums_s = dot(sq, sum_weights(None, 3))
    u = p * jnp.where(first, 2.0 ** -17, 2.0 ** -6) - sw * (2.0 ** -12)
    u_hi = u.astype(BF16)
    e1 = jnp.where(first, p * (1.0 / 64), 0.0).astype(BF16)
    e2 = pick3(sums_e) + (lane < 3).astype(F32)
    s2 = pick3(sums_s) + ((lane >= 6) & (lane < 9)).astype(F32) + jnp.where(lane == 9, 33.0 / 2048, 0.0)
    s2 = jnp.where(first, s2, u - u_hi.astype(F32))
    ref.b_op[quarter, 0:QCOLS, :] = jnp.concatenate([e1, e2.astype(BF16)], axis=1)
    ref.b_op[quarter, QCOLS:2 * QCOLS, :] = jnp.concatenate([u_hi, s2.astype(BF16)], axis=1)
    sw64 = sw * (-1.0 / 64)
    f1a = jnp.where(first, sw64, p)
    f1b = jnp.where(first, (lane == 0).astype(F32), sw64)
    f2a = jnp.where(first, p, 0.0)
    f2b = jnp.broadcast_to((lane == 1).astype(F32), p.shape)
    ref.f1[quarter] = jnp.concatenate([f1a, f1b], axis=1).astype(BF16)
    ref.f2[quarter] = jnp.concatenate([f2a, f2b], axis=1).astype(BF16)
    ref.colt[quarter] = p.T


def pair_weights(ref, town, row, col, zh):
    zl, y = col // 16, lax.rem(col // 2, 8)
    lane = lanes()
    k12 = ((lane // 2).astype(F32) < town).astype(F32)
    half = (row // 2).astype(F32)
    ln2 = 0.6931471805599453
    hi = float(ml_dtypes.bfloat16(ln2))
    mid = float(ml_dtypes.bfloat16(ln2 - hi))
    lo = ln2 - hi - mid
    ref.table[...] = jnp.zeros_like(ref.table)
    for t, offset in enumerate(OFFSETS):
        for core in range(2):
            g = 2 * t + core
            if offset[2]:
                weight = k12
            else:
                chip = chip_at(zl, y, offset, 1)
                k21 = (half < ref.t2[2 * chip + core]).astype(F32)
                weight = k12 + k21
            two = weight > 1.5
            ref.table[10 + g:11 + g, :] = jnp.where(weight < 0.5, BIG, jnp.where(two, hi, 0.0))
            ref.table[10 + RG + g:11 + RG + g, :] = jnp.where(two, mid, 0.0)
            ref.table[10 + 2 * RG + g:11 + 2 * RG + g, :] = jnp.where(two, lo, 0.0)
    table = ref.table[...].astype(BF16)

    def body(quarter, carry):
        x = lax.broadcasted_iota(jnp.int32, (QCOLS, 128), 0) // M
        zq = lax.rem(zh + quarter + 1, 4)
        hot = (lax.broadcasted_iota(jnp.int32, (QCOLS, 128), 1) == zq * 4 + x).astype(F32).astype(BF16)
        logs = dot_nt(hot, table).astype(BF16)
        ref.b_op[quarter, 0:QCOLS, 128:256] = ref.b_op[quarter, 0:QCOLS, 128:256] + logs
        return carry

    lax.fori_loop(0, QUART, body, 0)


def pair_step(ref, step, quarter):
    a = ref.a_op[pl.ds(step * RROWS, RROWS), :]
    es = dot_nt(a, ref.b_op[quarter])
    kept = jnp.exp(es[:, :QCOLS])
    coef = kept * es[:, QCOLS:]
    kb, cb = kept.astype(BF16), coef.astype(BF16)
    ref.racc[pl.ds(step * RROWS, RROWS), :] += dot(kb, ref.f1[quarter]) + dot(cb, ref.f2[quarter])
    ref.c1[quarter] += dot(ref.f1t[step], kb)
    ref.c2[quarter] += dot(ref.f2t[step], cb)


def finish_rows(ref, step):
    acc = ref.racc[pl.ds(step * RROWS, RROWS), :]
    low, high = acc[:, :128], acc[:, 128:]
    ks, cs = high[:, 0:1], high[:, 1:2]
    p = ref.rowbuf[pl.ds(step * RS_GROUPS, RS_GROUPS)].reshape(RROWS, 128).astype(F32)
    sw = pltpu.roll(p, 64, 1)
    grad = low + jnp.where(lanes() < 64, p * (-cs), high) + sw * (ks * (1.0 / 64))
    grad = grad.reshape(RS_GROUPS, M, 128)
    ref.rsend[pl.ds(step * RS_GROUPS, RS_GROUPS)] = grad.astype(BF16)
    ref.rowg[...] = grad
    ref.lossv[...] += jnp.sum(high, axis=0, keepdims=True)


def finish_cols(ref, quarter):
    g1, g2 = ref.c1[quarter], ref.c2[quarter]
    pt = ref.colt[quarter]
    xt, st = pt[0:64], pt[64:128]
    ks = g1[192:193] * (1.0 / 64)
    cs = g2[64:65]
    gx = g2[0:64] + g1[0:64] - xt * cs + st * ks
    gs = g1[64:128] + g1[128:192] + xt * ks
    grad = jnp.concatenate([gx, gs], axis=0).T.reshape(4, M, 128)
    ref.csend[pl.ds(quarter * 4, 4)] = grad.astype(BF16)
    ref.colg[...] = grad


def chip_at(zl, y, offset, sign):
    other, dy, _ = offset
    z = lax.rem(zl + other, 2)
    if dy is None:
        from_z = zl if sign > 0 else z
        dy = 4 * from_z
    return z * 8 + lax.rem(y + sign * dy + 16, 8)


class Refs:
    def __init__(self, names, refs):
        for name, r in zip(names, refs):
            setattr(self, name, r)


SCRATCH = dict(
    own=pltpu.VMEM((M, 128), BF16),
    rowbuf=pltpu.VMEM((RG, M, 128), BF16),
    colbuf=pltpu.VMEM((NROW, M, 128), BF16),
    t1=pltpu.VMEM((NROW, 1, 128), F32),
    t2=pltpu.VMEM((NCOL, 1, 128), F32),
    tsrc=pltpu.VMEM((1, 128), F32),
    tvec=pltpu.VMEM((1, 128), F32),
    table=pltpu.VMEM((128, 128), F32),
    a_op=pltpu.VMEM((RG * M, 256), BF16),
    b_op=pltpu.VMEM((QUART, 2 * QCOLS, 256), BF16),
    f1=pltpu.VMEM((QUART, QCOLS, 256), BF16),
    f2=pltpu.VMEM((QUART, QCOLS, 256), BF16),
    f1t=pltpu.VMEM((SUPER, 208, RROWS), BF16),
    f2t=pltpu.VMEM((SUPER, 80, RROWS), BF16),
    colt=pltpu.VMEM((QUART, 128, QCOLS), F32),
    racc=pltpu.VMEM((RG * M, 256), F32),
    c1=pltpu.VMEM((QUART, 208, QCOLS), F32),
    c2=pltpu.VMEM((QUART, 80, QCOLS), F32),
    rsend=pltpu.VMEM((RG, M, 128), BF16),
    csend=pltpu.VMEM((NROW, M, 128), BF16),
    rowg=pltpu.VMEM((RS_GROUPS, M, 128), F32),
    colg=pltpu.VMEM((4, M, 128), F32),
    rrow=pltpu.VMEM((RG, M, 128), BF16),
    rcol=pltpu.VMEM((NROW, M, 128), BF16),
    lossv=pltpu.VMEM((1, 128), F32),
    lsum=pltpu.VMEM((1, 128), F32),
    la=pltpu.VMEM((NCOL, 1, 128), F32),
    lb=pltpu.VMEM((NROW, 1, 128), F32),
)
SEMS = dict(
    t1=NROW, t2=NCOL, col=NROW, row=RG, rr=RG, rc=NROW, la=NCOL, lb=NROW,
)


def kernel(samples, scores, groups, out_x, out_s, out_loss, *rest):
    ref = Refs(SCRATCH, rest[:len(SCRATCH)])
    sems = rest[len(SCRATCH):]
    send = Refs(SEMS, sems[:len(SEMS)])
    recv = Refs(SEMS, sems[len(SEMS):])
    row, col = lax.axis_index("row"), lax.axis_index("col")
    zh, x = row // 4, lax.rem(row, 4)
    zl, y, core = col // 16, lax.rem(col // 2, 8), lax.rem(col, 2)
    sib = col + 1 - 2 * core

    barrier = pltpu.get_barrier_semaphore()

    def greet_col(d, carry):
        pl.semaphore_signal(barrier, inc=1, device_id=(lax.rem(row + d, NROW), col), device_id_type=MESH)
        return carry

    def greet_row(d, carry):
        pl.semaphore_signal(barrier, inc=1, device_id=(row, lax.rem(col + d, NCOL)), device_id_type=MESH)
        return carry

    lax.fori_loop(1, NROW, greet_col, 0)
    lax.fori_loop(1, NCOL, greet_row, 0)

    own = jnp.concatenate([samples[...], scores[...]], axis=1)
    ref.own[...] = own
    ref.rowbuf[2 * (CHUNKS - 1) + core] = own
    ref.colbuf[12 + x] = own
    town = groups[0, 0].astype(F32)
    tfull = jnp.full((1, 128), town, F32)
    ref.tsrc[...] = tfull
    ref.t1[row] = tfull
    ref.racc[...] = jnp.zeros_like(ref.racc)
    ref.c1[...] = jnp.zeros_like(ref.c1)
    ref.c2[...] = jnp.zeros_like(ref.c2)
    ref.lossv[...] = jnp.zeros_like(ref.lossv)

    pl.semaphore_wait(barrier, NROW + NCOL - 2)

    def copy(src, dst, ssem, rsem, to_row, to_col):
        return pltpu.make_async_remote_copy(
            src_ref=src, dst_ref=dst, send_sem=ssem, recv_sem=rsem,
            device_id=(to_row, to_col), device_id_type=MESH,
        )

    def t1_copy(d):
        return copy(ref.tsrc, ref.t1.at[row], send.t1.at[d], recv.t1.at[row], lax.rem(row + d, NROW), col)

    def t2_copy(d):
        return copy(ref.tvec, ref.t2.at[col], send.t2.at[d], recv.t2.at[col], row, lax.rem(col + d, NCOL))

    def z_copy(d):
        slot = (3 - d) * 4 + x
        return copy(ref.own, ref.colbuf.at[slot], send.col.at[d], recv.col.at[slot],
                    lax.rem(zh + d, 4) * 4 + x, col)

    def x_copy(quarter, d):
        slot = quarter * 4 + x
        src = ref.own if quarter == 3 else ref.colbuf.at[slot]
        return copy(src, ref.colbuf.at[slot], send.col.at[4 + 3 * quarter + d - 1], recv.col.at[slot],
                    zh * 4 + lax.rem(x + d, 4), col)

    def row_copy(t):
        chip = chip_at(zl, y, OFFSETS[t], -1)
        slot = 2 * t + core
        return copy(ref.own, ref.rowbuf.at[slot], send.row.at[t], recv.row.at[slot], row, 2 * chip + core)

    def sib_copy(t):
        slot = 2 * t + core
        src = ref.own if t == CHUNKS - 1 else ref.rowbuf.at[slot]
        return copy(src, ref.rowbuf.at[slot], send.row.at[CHUNKS - 1 + t], recv.row.at[slot], row, sib)

    def rr_copy(t, b):
        if t == CHUNKS - 1:
            return copy(ref.rsend.at[2 * t + 1 - core], ref.rrow.at[2 * t + core], send.rr.at[2 * t],
                        recv.rr.at[2 * t + core], row, sib)
        chip = chip_at(zl, y, OFFSETS[t], 1)
        slot = 2 * t + core
        return copy(ref.rsend.at[2 * t + b], ref.rrow.at[slot], send.rr.at[2 * t + b], recv.rr.at[slot],
                    row, 2 * chip + b)

    def rc_copy(quarter, k):
        if quarter == 3:
            xs = lax.rem(x + k, 4)
            to = zh * 4 + xs
            sem = 12 + k
        else:
            xs = k
            to = lax.rem(zh + quarter + 1, 4) * 4 + xs
            sem = quarter * 4 + k
        there = lax.rem(row - to + NROW, NROW)
        return copy(ref.csend.at[quarter * 4 + xs], ref.rcol.at[there], send.rc.at[sem], recv.rc.at[there], to, col)

    def la_copy(d):
        return copy(ref.lossv, ref.la.at[col], send.la.at[d], recv.la.at[col], row, lax.rem(col + d, NCOL))

    def lb_copy(d):
        return copy(ref.lsum, ref.lb.at[row], send.lb.at[d], recv.lb.at[row], lax.rem(row + d, NROW), col)

    def each(start, stop, act):
        def body(d, carry):
            act(d)
            return carry
        lax.fori_loop(start, stop, body, 0)

    def landed(buf, sem, slot):
        copy(buf.at[slot], buf.at[slot], sem.at[slot], sem.at[slot], row, sib).wait_recv()

    for d in range(1, 4):
        z_copy(d).start()
    each(1, NROW, lambda d: t1_copy(d).start())
    for t in range(CHUNKS - 1):
        row_copy(t).start()
    for d in range(1, 4):
        x_copy(3, d).start()
    sib_copy(CHUNKS - 1).start()

    for quarter in range(3):
        landed(ref.colbuf, recv.col, quarter * 4 + x)
        for d in range(1, 4):
            x_copy(quarter, d).start()

    each(1, NROW, lambda d: landed(ref.t1, recv.t1, lax.rem(row + d, NROW)))
    lane3 = lax.broadcasted_iota(jnp.int32, (NROW, 1, 128), 2)
    slot3 = lax.broadcasted_iota(jnp.int32, (NROW, 1, 128), 0)
    tvec = jnp.sum(jnp.where(lane3 == slot3, ref.t1[...], 0.0), axis=0)
    ref.tvec[...] = tvec
    ref.t2[col] = tvec
    each(1, NCOL, lambda d: t2_copy(d).start())

    for t in range(CHUNKS - 1):
        landed(ref.rowbuf, recv.row, 2 * t + core)
        sib_copy(t).start()

    each(1, 4, lambda d: landed(ref.colbuf, recv.col, 12 + lax.rem(x + d, 4)))
    for quarter in range(3):
        for d in range(1, 4):
            landed(ref.colbuf, recv.col, quarter * 4 + lax.rem(x + d, 4))
    each(0, QUART, lambda quarter: prep_cols(ref, quarter))
    each(0, CHUNKS, lambda t: landed(ref.rowbuf, recv.row, 2 * t + 1 - core))
    each(0, SUPER, lambda step: prep_rows(ref, step))
    each(1, NCOL, lambda d: landed(ref.t2, recv.t2, lax.rem(col + d, NCOL)))
    pair_weights(ref, town, row, col, zh)

    for quarter in range(3):
        each(0, SUPER, lambda step: pair_step(ref, step, quarter))
        finish_cols(ref, quarter)
        for k in range(4):
            rc_copy(quarter, k).start()
    for step in range(SUPER):
        pair_step(ref, step, 3)
        finish_rows(ref, step)
        for t in range(3 * step, 3 * step + 3):
            for b in range(1 if t == CHUNKS - 1 else 2):
                rr_copy(t, b).start()

    lane = lanes()
    own32 = ref.own[...].astype(F32)
    kept_diag = ((row // 2).astype(F32) < jnp.full((1, 128), town, F32)).astype(F32)
    loss_lanes = jnp.where(lane == 0, -1.0 / 32, jnp.where(lane == 1, 64.0, 0.0))
    s2 = jnp.sum(jnp.where(lane < 64, 1.0 / 64, own32 * own32 * (1.0)), axis=0, keepdims=True)
    ref.lossv[...] = ref.lossv[...] * loss_lanes - kept_diag * s2
    ref.la[col] = ref.lossv[...]
    each(1, NCOL, lambda d: la_copy(d).start())

    finish_cols(ref, 3)
    for k in range(1, 4):
        rc_copy(3, k).start()

    t2 = ref.t2[...]
    lane_n = lax.broadcasted_iota(jnp.int32, (NCOL, 1, 128), 2)
    diag = ((lane_n // 2).astype(F32) < t2).astype(F32)
    pairs = jnp.sum(jnp.sum(t2 * (128.0 * 2048.0) - 64.0 * diag, axis=0), axis=1, keepdims=True)
    scale = EVERYONE / pairs

    each(1, NCOL, lambda d: landed(ref.la, recv.la, lax.rem(col + d, NCOL)))
    lsum = jnp.sum(ref.la[...], axis=0)
    ref.lsum[...] = lsum
    ref.lb[row] = lsum
    each(1, NROW, lambda d: lb_copy(d).start())

    total = ref.rowg[2 * (CHUNKS - 1) - RS_GROUPS * (SUPER - 1) + core] + ref.colg[x]
    total = total - jnp.where(lane < 64, 0.0, 2.0 * kept_diag * own32)
    each(0, CHUNKS - 1, lambda t: (landed(ref.rrow, recv.rr, 2 * t), landed(ref.rrow, recv.rr, 2 * t + 1)))
    landed(ref.rrow, recv.rr, 2 * (CHUNKS - 1) + 1 - core)
    total = total + jnp.sum(ref.rrow[0:RG - 2].astype(F32), axis=0)
    total = total + ref.rrow[2 * (CHUNKS - 1) + 1 - core].astype(F32)
    each(1, NROW, lambda d: landed(ref.rcol, recv.rc, d))
    total = total + jnp.sum(ref.rcol[1:NROW].astype(F32), axis=0)
    total = total * scale
    out_x[...] = total[:, :64]
    out_s[...] = total[:, 64:]

    each(1, NROW, lambda d: landed(ref.lb, recv.lb, lax.rem(row + d, NROW)))
    out_loss[...] = jnp.sum(jnp.sum(ref.lb[...], axis=0), axis=1, keepdims=True) / pairs

    for d in range(1, 4):
        z_copy(d).wait_send()
    for quarter in range(QUART):
        for d in range(1, 4):
            x_copy(quarter, d).wait_send()
    for t in range(CHUNKS - 1):
        row_copy(t).wait_send()
    for t in range(CHUNKS):
        sib_copy(t).wait_send()
    for t in range(CHUNKS):
        for b in range(1 if t == CHUNKS - 1 else 2):
            rr_copy(t, b).wait_send()
    for quarter in range(QUART):
        for k in range(1 if quarter == 3 else 0, 4):
            rc_copy(quarter, k).wait_send()
    each(1, NROW, lambda d: t1_copy(d).wait_send())
    each(1, NCOL, lambda d: t2_copy(d).wait_send())
    each(1, NCOL, lambda d: la_copy(d).wait_send())
    each(1, NROW, lambda d: lb_copy(d).wait_send())


def shards(samples, scores, tile_groups):
    vmem = pl.BlockSpec(memory_space=pltpu.VMEM)
    out_x, out_s, loss = pl.pallas_call(
        kernel,
        out_shape=(
            jax.ShapeDtypeStruct((M, 64), F32),
            jax.ShapeDtypeStruct((M, 64), F32),
            jax.ShapeDtypeStruct((1, 1), F32),
        ),
        in_specs=[vmem, vmem, pl.BlockSpec(memory_space=pltpu.SMEM)],
        out_specs=(vmem, vmem, vmem),
        scratch_shapes=list(SCRATCH.values())
        + [pltpu.SemaphoreType.DMA((n,)) for n in SEMS.values()] * 2,
        compiler_params=pltpu.CompilerParams(
            collective_id=0, has_side_effects=True, vmem_limit_bytes=40 * 2**20
        ),
    )(samples, scores, tile_groups)
    return out_x, out_s, loss[0, 0]


def solution(mesh):
    placed = (P(("row", "col"), None), P(("row", "col"), None), P("row", "col"))
    return jax.shard_map(
        shards,
        mesh=mesh,
        in_specs=placed,
        out_specs=(P(("row", "col"), None), P(("row", "col"), None), P()),
        check_vma=False,
    )
```

time: 387 us -> 61 us (0.16)
  blocking collectives: 185 us -> 0 us
  waiting for transfers between devices: 98.6 us -> 0 us
  Pallas kernels: 0 us -> 55 us
  matrix products: 41.8 us -> 0 us
  local copies, waits for them, and re-layouts: 17.6 us -> 2.66 us
  between operations: 17.2 us -> 3.06 us
  other arithmetic: 12.1 us -> 0 us
  loops' own time: 11.2 us -> 0 us
    psum x1 -> x0, blocking collectives: 101 us -> none  [shards(): total, pairs = lax.psum((loss_sum, count_sum), ('row', 'col'))]
    reduce_scatter x2 -> x0, waiting for transfers between devices: 98.6 us -> none  [the longest x1 98.6 us: shards(): lax.psum_scatter(row_acc, 'col', scatter_dimension=0, tiled=True)]
    all_gather x2 -> x0, blocking collectives: 83.4 us -> none  [the longest x1 44.9 us: shards(): cols = lax.all_gather(local_pair, 'row', axis=0, tiled=True)]
    pallas_call x0 -> x1, Pallas kernels: none -> 55 us  [shards(): pl.pallas_call(kernel, out_shape=(jax.ShapeDtypeStruct((M, 64), F32), jax...]
    dot_general x64 -> x0, matrix products: 41.8 us -> none  [the longest x8 14.9 us: tile_terms(): g_xs = jnp.dot(x_rows, s_cols.T, preferred_element_type=jnp.float32)]
    another operation x1 -> x0, loops' own time: 11.2 us -> none  [shards(): lax.fori_loop(0, number, accumulate, init)]
    while x25 -> x0, local copies, waits for them, and re-layouts: 10.1 us -> none
    dynamic_update_slice x16 -> x0, local copies, waits for them, and re-layouts: 5.72 us -> none  [accumulate(): col_acc = lax.dynamic_update_slice_in_dim(col_acc, col_grad, start, 0)]
  transfers between devices with their start and end apart: 2 -> 0, of which waited for: 1 -> 0; matrix products, arithmetic and copies ran while one was open for 0% -> 0% of each run, Pallas kernels for 0% -> 0%
where the time goes in v1:
time: 61 us; the launch traced here: 60.7 us
  Pallas kernels  55 us (90%)
  between operations  3.06 us (5%)
  local copies, waits for them, and re-layouts  2.66 us (4%)
    pallas_call x1, Pallas kernels, shards(): pl.pallas_call(kernel, out_shape=(jax.ShapeDtypeStruct((M, 64), F32), jax...  55 us
    unnamed x6, local copies, waits for them, and re-layouts  2.66 us

profile of v1, /device:TPU:1, one launch (start us, length us, event | category | flops | bytes accessed | tf_op | source)
XLA Modules:
  0.0 60.7 jit_solution(17515375730270972488)
XLA Ops:
  1.3 0.0 copy-start
  1.3 0.7 %copy-done = bf16[64,64]{1,0:T(8,128)(2,1)S(1)} copy-done((bf16[64,64]{1,0:T(8,128)(2,1)S(1)}, bf16[64,64]{1,0:T(8,128)(2,1)}, u32[]{:S(2)}) %copy-start) | copy-done | bytes 8216
  2.0 0.0 copy-start.1
  2.0 0.7 %copy-done.1 = bf16[64,64]{1,0:T(8,128)(2,1)S(1)} copy-done((bf16[64,64]{1,0:T(8,128)(2,1)S(1)}, bf16[64,64]{1,0:T(8,128)(2,1)}, u32[]{:S(2)}) %copy-start.1) | copy-done | bytes 8216
  2.7 55.0 %shard_map.58 = (f32[64,64]{1,0:T(8,128)S(1)}, f32[64,64]{1,0:T(8,128)S(1)}, f32[1,1]{1,0:T(1,128)}) custom-call(bf16[64,64]{1,0:T(8,128)(2,1)S(1)} %copy-done, bf16[64,64]{1,0:T(8,128)(2,1)S(1)} %copy-done.1, s32[1,1]{1,0:T(1,128)S(6)} %copy.9.groups), custom_call_target="tpu_custom_call" | custom-call | tf_op jit(solution)/shard_map/pallas_call | solution.py:464
  57.8 0.6 %copy.10 = f32[64,64]{1,0:T(8,128)} copy(f32[64,64]{1,0:T(8,128)S(1)} %get-tuple-element.12) | data formatting | bytes 32768
  58.4 0.6 %copy.11 = f32[64,64]{1,0:T(8,128)} copy(f32[64,64]{1,0:T(8,128)S(1)} %get-tuple-element.13) | data formatting | bytes 32768
Async XLA Ops:
  1.3 0.7 %copy-start = (bf16[64,64]{1,0:T(8,128)(2,1)S(1)}, bf16[64,64]{1,0:T(8,128)(2,1)}, u32[]{:S(2)}) copy-start(bf16[64,64]{1,0:T(8,128)(2,1)} %samples.1) | copy-start | bytes 24580
  2.0 0.7 %copy-start.1 = (bf16[64,64]{1,0:T(8,128)(2,1)S(1)}, bf16[64,64]{1,0:T(8,128)(2,1)}, u32[]{:S(2)}) copy-start(bf16[64,64]{1,0:T(8,128)(2,1)} %scores.1) | copy-start | bytes 24580

commit v2 on v1

v2 whole, which is shorter than its diff:
```python
import jax
import jax.numpy as jnp
from jax import lax
from jax.experimental import pallas as pl
from jax.experimental.pallas import tpu as pltpu
from jax.sharding import PartitionSpec as P

MESH = pl.DeviceIdType.MESH
F32 = jnp.float32
BF16 = jnp.bfloat16

NROW, NCOL = 16, 32
M = 64
CHUNKS = 9
RG = 2 * CHUNKS
SUPER = 3
GROUPS = RG // SUPER
ROWS = GROUPS * M
QUART = 4
QCOLS = 4 * M
EVERYONE = float(M * NROW * NCOL)
NSLOT = 14

OFFSETS = (
    (0, 4, True), (0, 3, False), (1, -3, False),
    (1, None, False), (1, 2, False), (0, -2, False),
    (0, 1, False), (1, -1, False), (0, 0, True),
)


def split3(value):
    hi = value.astype(BF16).astype(F32)
    rest = value - hi
    mid = rest.astype(BF16).astype(F32)
    return hi, mid, rest - mid


def dot(a, b):
    return lax.dot_general(a, b, (((1,), (0,)), ((), ())), preferred_element_type=F32)


def dot_nt(a, b):
    return lax.dot_general(a, b, (((1,), (1,)), ((), ())), preferred_element_type=F32)


def lanes(rows=1, width=128):
    return lax.broadcasted_iota(jnp.int32, (rows, width), 1)


def squares(p, sw):
    q = p * jnp.where(lanes() < 64, p, sw)
    hi = q.astype(BF16)
    return jnp.concatenate([hi, (q - hi.astype(F32)).astype(BF16)], axis=1)


def sum_weights(e_lanes, s_lanes):
    k = lax.broadcasted_iota(jnp.int32, (256, 128), 0) % 128
    lane = lax.broadcasted_iota(jnp.int32, (256, 128), 1)
    is_x = k < 64
    out = jnp.zeros((256, 128), F32)
    if e_lanes is not None:
        in_e = (lane >= e_lanes) & (lane < e_lanes + 3)
        out = jnp.where(in_e & is_x, -(2.0 ** -7), out)
    if s_lanes is not None:
        in_s = (lane >= s_lanes) & (lane < s_lanes + 3)
        out = jnp.where(in_s, jnp.where(is_x, -(2.0 ** -18), 2.0 ** -12), out)
    return out.astype(BF16)


def pick3(value):
    hi, mid, lo = split3(value)
    part = lanes() % 3
    return jnp.where(part == 0, hi, jnp.where(part == 1, mid, lo))


def prep_rows(ref, step):
    pair = ref.rowbuf[pl.ds(step * GROUPS, GROUPS)].reshape(ROWS, 128)
    p = pair.astype(F32)
    sw = pltpu.roll(p, 64, 1)
    lane = lanes()
    sums = dot(squares(p, sw), sum_weights(0, 6))
    one = (((lane >= 3) & (lane < 6)) | (lane == 9)).astype(F32)
    misc = pick3(sums) + one
    ext = jnp.where(lane < 64, misc, p).astype(BF16)
    ref.a_op[step] = jnp.concatenate([pair, ext], axis=1)
    pt = p.T
    xt, st = pt[0:64], pt[64:128]
    ones = jnp.ones((16, ROWS), F32)
    at = pl.ds(step * ROWS, ROWS)
    ref.f1t[:, at] = jnp.concatenate([st * (-1.0 / 64), st, xt * (-1.0 / 64), ones], axis=0).astype(BF16)
    ref.f2t[:, at] = jnp.concatenate([xt, ones], axis=0).astype(BF16)


def prep_cols(ref, quarter):
    pair = ref.colbuf[pl.ds(quarter * 4, 4)].reshape(QCOLS, 128)
    p = pair.astype(F32)
    sw = pltpu.roll(p, 64, 1)
    lane = lanes()
    first = lane < 64
    sq = squares(p, sw)
    sums_e = dot(sq, sum_weights(3, None))
    sums_s = dot(sq, sum_weights(None, 3))
    u = p * jnp.where(first, 2.0 ** -17, 2.0 ** -6) - sw * (2.0 ** -12)
    u_hi = u.astype(BF16)
    e1 = jnp.where(first, p * (1.0 / 64), 0.0).astype(BF16)
    e2 = pick3(sums_e) + (lane < 3).astype(F32)
    s2 = pick3(sums_s) + ((lane >= 6) & (lane < 9)).astype(F32) + jnp.where(lane == 9, 33.0 / 2048, 0.0)
    s2 = jnp.where(first, s2, u - u_hi.astype(F32))
    ref.b_op[quarter, 0:QCOLS, :] = jnp.concatenate([e1, e2.astype(BF16)], axis=1)
    ref.b_op[quarter, QCOLS:2 * QCOLS, :] = jnp.concatenate([u_hi, s2.astype(BF16)], axis=1)
    sw64 = sw * (-1.0 / 64)
    f1a = jnp.where(first, sw64, p)
    f1b = jnp.where(first, (lane == 0).astype(F32), sw64)
    f2a = jnp.where(first, p, 0.0)
    f2b = jnp.broadcast_to((lane == 1).astype(F32), p.shape)
    at = pl.ds(quarter * QCOLS, QCOLS)
    ref.f1[at, :] = jnp.concatenate([f1a, f1b], axis=1).astype(BF16)
    ref.f2[at, :] = jnp.concatenate([f2a, f2b], axis=1).astype(BF16)
    ref.colt[quarter] = p.T


def pair_step(ref, step, quarter):
    es = dot_nt(ref.a_op[step], ref.b_op[quarter])
    kept = jnp.exp(es[:, :QCOLS])
    coef = kept * es[:, QCOLS:]
    at = (pl.ds(step * ROWS, ROWS), slice(quarter * QCOLS, (quarter + 1) * QCOLS))
    ref.kmat[at] = kept.astype(BF16)
    ref.cmat[at] = coef.astype(BF16)
    to = (step, slice(0, GROUPS), slice(quarter * QCOLS, (quarter + 1) * QCOLS))
    ref.usum[to] = jnp.sum((coef * 64.0 - kept * (1.0 / 32)).reshape(GROUPS, M, QCOLS), axis=1)


def expansion(ref, row, zh, x):
    lane = lanes(1, NROW * M)
    slot = lane // M
    quarter, dx = slot // 4, slot % 4
    other = ((zh + quarter + 1) % 4) * 4 + (x + dx) % 4
    place = (other - row + NROW) % NROW
    hot = (lax.broadcasted_iota(jnp.int32, (NROW, NROW * M), 0) == place).astype(F32)
    ref.spread[...] = jnp.concatenate([hot, jnp.zeros((128 - NROW, NROW * M), F32)], axis=0).astype(BF16)


def pair_weights(ref, town, row):
    lane = lanes()
    theirs = ((row + lane) % NROW) // 2
    k12 = (theirs.astype(F32) < town).astype(F32)
    half = (row // 2).astype(F32)
    ref.table[...] = jnp.zeros_like(ref.table)
    for step in range(SUPER):
        for i in range(GROUPS):
            rel, t = i // 3, 3 * step + i % 3
            weight = k12
            if not OFFSETS[t][2]:
                weight = k12 + (half < ref.t2[2 * (t - 1) + rel]).astype(F32)
            ref.table[8 * step + i:8 * step + i + 1, :] = weight
    ref.wtab[...] = dot(ref.table[...].astype(BF16), ref.spread[...]).reshape(4, 8, NROW * M)


def weighted(mat, ref, step, start, width):
    at = slice(start, start + width)
    out = []
    for i in range(GROUPS):
        w = jnp.broadcast_to(ref.wtab[step, i:i + 1, at], (16, width)).astype(BF16)
        part = mat[step * ROWS + i * M:step * ROWS + (i + 1) * M, at]
        out.append(part * jnp.concatenate([w] * (M // 16), axis=0))
    return jnp.concatenate(out, axis=0)


def row_results(ref, step):
    kb = weighted(ref.kmat, ref, step, 0, NROW * M)
    cb = weighted(ref.cmat, ref, step, 0, NROW * M)
    acc = dot(kb, ref.f1[...]) + dot(cb, ref.f2[...])
    low, high = acc[:, :128], acc[:, 128:]
    ks, cs = high[:, 0:1], high[:, 1:2]
    p = ref.rowbuf[step * GROUPS:(step + 1) * GROUPS].reshape(ROWS, 128).astype(F32)
    sw = pltpu.roll(p, 64, 1)
    grad = low + jnp.where(lanes() < 64, p * (-cs), high) + sw * (ks * (1.0 / 64))
    grad = grad.reshape(GROUPS, M, 128)
    ref.rowg[step] = grad[0:3]
    ref.sibsend[step] = grad[3:6].astype(BF16)


def col_results(ref, quarter):
    kb = jnp.concatenate([weighted(ref.kmat, ref, s, quarter * QCOLS, QCOLS) for s in range(SUPER)], axis=0)
    cb = jnp.concatenate([weighted(ref.cmat, ref, s, quarter * QCOLS, QCOLS) for s in range(SUPER)], axis=0)
    g1 = dot(ref.f1t[...], kb)
    g2 = dot(ref.f2t[...], cb)
    pt = ref.colt[quarter]
    xt, st = pt[0:64], pt[64:128]
    ks = g1[192:193] * (1.0 / 64)
    cs = g2[64:65]
    gx = g2[0:64] + g1[0:64] - xt * cs + st * ks
    gs = g1[64:128] + g1[128:192] + xt * ks
    grad = jnp.concatenate([gx, gs], axis=0).T.reshape(4, M, 128)
    ref.csend[quarter * 4:quarter * 4 + 4] = grad.astype(BF16)
    if quarter == 3:
        ref.colown[...] = grad[0]


def chip_at(zl, y, offset, sign):
    other, dy, _ = offset
    z = lax.rem(zl + other, 2)
    if dy is None:
        from_z = zl if sign > 0 else z
        dy = 4 * from_z
    return z * 8 + lax.rem(y + sign * dy + 16, 8)


class Refs:
    def __init__(self, names, refs):
        for name, r in zip(names, refs):
            setattr(self, name, r)


SCRATCH = dict(
    xin=pltpu.VMEM((M, 64), BF16),
    sin=pltpu.VMEM((M, 64), BF16),
    own=pltpu.VMEM((M, 128), BF16),
    rowbuf=pltpu.VMEM((RG, M, 128), BF16),
    colbuf=pltpu.VMEM((NROW, M, 128), BF16),
    t1=pltpu.VMEM((NROW, 1, 128), F32),
    t2=pltpu.VMEM((NSLOT, 1, 128), F32),
    tsrc=pltpu.VMEM((1, 128), F32),
    tvec=pltpu.VMEM((1, 128), F32),
    table=pltpu.VMEM((32, 128), F32),
    spread=pltpu.VMEM((128, NROW * M), BF16),
    wtab=pltpu.VMEM((4, 8, NROW * M), F32),
    a_op=pltpu.VMEM((SUPER, ROWS, 256), BF16),
    b_op=pltpu.VMEM((QUART, 2 * QCOLS, 256), BF16),
    f1=pltpu.VMEM((NROW * M, 256), BF16),
    f2=pltpu.VMEM((NROW * M, 256), BF16),
    f1t=pltpu.VMEM((208, RG * M), BF16),
    f2t=pltpu.VMEM((80, RG * M), BF16),
    colt=pltpu.VMEM((QUART, 128, QCOLS), F32),
    kmat=pltpu.VMEM((RG * M, NROW * M), BF16),
    cmat=pltpu.VMEM((RG * M, NROW * M), BF16),
    usum=pltpu.VMEM((SUPER, 8, NROW * M), F32),
    rowg=pltpu.VMEM((SUPER, 3, M, 128), F32),
    sibsend=pltpu.VMEM((SUPER, 3, M, 128), BF16),
    sibrecv=pltpu.VMEM((SUPER, 3, M, 128), BF16),
    rsend=pltpu.VMEM((CHUNKS - 1, M, 128), BF16),
    csend=pltpu.VMEM((NROW, M, 128), BF16),
    rowown=pltpu.VMEM((M, 128), F32),
    colown=pltpu.VMEM((M, 128), F32),
    rrow=pltpu.VMEM((CHUNKS - 1, M, 128), BF16),
    rcol=pltpu.VMEM((NROW - 1, M, 128), BF16),
    lossv=pltpu.VMEM((1, 128), F32),
    lsum=pltpu.VMEM((1, 128), F32),
    la=pltpu.VMEM((NCOL, 1, 128), F32),
    lb=pltpu.VMEM((NROW, 1, 128), F32),
)
SEND = dict(load=2, t1=1, t2=1, col=1, row=1, sib=1, sg=1, rr=1, rc=1, la=1, lb=1)
RECV = dict(t1=1, t2=1, col=QUART, row=SUPER, sib=SUPER, sg=SUPER, rr=1, rc=1, la=1, lb=1)


def kernel(samples, scores, groups, out_x, out_s, out_loss, *rest):
    ref = Refs(SCRATCH, rest[:len(SCRATCH)])
    sems = rest[len(SCRATCH):]
    send = Refs(SEND, sems[:len(SEND)])
    recv = Refs(RECV, sems[len(SEND):])
    row, col = lax.axis_index("row"), lax.axis_index("col")
    zh, x = row // 4, lax.rem(row, 4)
    zl, y, core = col // 16, lax.rem(col // 2, 8), lax.rem(col, 2)
    sib = col + 1 - 2 * core

    def each(start, stop, act):
        def body(d, carry):
            act(d)
            return carry
        lax.fori_loop(start, stop, body, 0)

    barrier = pltpu.get_barrier_semaphore()

    def greet(to_row, to_col):
        pl.semaphore_signal(barrier, inc=1, device_id=(to_row, to_col), device_id_type=MESH)

    each(1, NROW, lambda d: greet(lax.rem(row + d, NROW), col))
    each(1, NCOL, lambda d: greet(row, lax.rem(col + d, NCOL)))

    loads = [pltpu.make_async_copy(samples, ref.xin, send.load.at[0]),
             pltpu.make_async_copy(scores, ref.sin, send.load.at[1])]
    for load in loads:
        load.start()
    town = groups[0, 0].astype(F32)
    tfull = jnp.full((1, 128), town, F32)
    ref.tsrc[...] = tfull
    ref.t1[0] = tfull
    expansion(ref, row, zh, x)
    for load in loads:
        load.wait()
    own = jnp.concatenate([ref.xin[...], ref.sin[...]], axis=1)
    ref.own[...] = own
    ref.rowbuf[RG - 4] = own
    ref.colbuf[12] = own
    pl.semaphore_wait(barrier, NROW + NCOL - 2)

    def copy(src, dst, ssem, rsem, to_row, to_col):
        return pltpu.make_async_remote_copy(
            src_ref=src, dst_ref=dst, send_sem=ssem, recv_sem=rsem,
            device_id=(to_row, to_col), device_id_type=MESH,
        )

    def t1_copy(d):
        return copy(ref.tsrc, ref.t1.at[NROW - d], send.t1.at[0], recv.t1.at[0], lax.rem(row + d, NROW), col)

    def t2_copy(t, b):
        chip = chip_at(zl, y, OFFSETS[t], -1)
        slot = 2 * (t - 1) + lax.rem(core + b, 2)
        return copy(ref.tvec, ref.t2.at[slot], send.t2.at[0], recv.t2.at[0], row, 2 * chip + b)

    def col_copy(quarter, dx):
        dz = (quarter + 1) % 4
        to = lax.rem(zh + 4 - dz, 4) * 4 + lax.rem(x + 4 - dx, 4)
        return copy(ref.own, ref.colbuf.at[quarter * 4 + dx], send.col.at[0], recv.col.at[quarter], to, col)

    def row_copy(t):
        chip = chip_at(zl, y, OFFSETS[t], -1)
        slot = GROUPS * (t // 3) + t % 3
        return copy(ref.own, ref.rowbuf.at[slot], send.row.at[0], recv.row.at[t // 3], row, 2 * chip + core)

    def sib_copy(step):
        at = GROUPS * step
        return copy(ref.rowbuf.at[at:at + 3], ref.rowbuf.at[at + 3:at + 6], send.sib.at[0], recv.sib.at[step], row, sib)

    def sg_copy(step):
        return copy(ref.sibsend.at[step], ref.sibrecv.at[step], send.sg.at[0], recv.sg.at[step], row, sib)

    def rr_copy(t):
        chip = chip_at(zl, y, OFFSETS[t], 1)
        return copy(ref.rsend.at[t], ref.rrow.at[t], send.rr.at[0], recv.rr.at[0], row, 2 * chip + core)

    def rc_copy(quarter, dx):
        dz = (quarter + 1) % 4
        to = lax.rem(zh + dz, 4) * 4 + lax.rem(x + dx, 4)
        slot = quarter * 4 + dx - (1 if quarter == 3 else 0)
        return copy(ref.csend.at[quarter * 4 + dx], ref.rcol.at[slot], send.rc.at[0], recv.rc.at[0], to, col)

    def la_copy(d):
        return copy(ref.lossv, ref.la.at[NCOL - d], send.la.at[0], recv.la.at[0], row, lax.rem(col + d, NCOL))

    def lb_copy(d):
        return copy(ref.lsum, ref.lb.at[NROW - d], send.lb.at[0], recv.lb.at[0], lax.rem(row + d, NROW), col)

    def landed(buf, sem):
        copy(buf, buf, sem, sem, row, sib).wait_recv()

    def left(buf, sem):
        copy(buf, buf, sem, sem, row, sib).wait_send()

    each(1, NROW, lambda d: t1_copy(d).start())
    for t in range(CHUNKS - 1):
        row_copy(t).start()
    for quarter in (1, 0, 2, 3):
        for dx in (2, 1, 3, 0):
            if (quarter, dx) != (3, 0):
                col_copy(quarter, dx).start()

    def got_cols(quarter):
        at = quarter * 4
        landed(ref.colbuf.at[at + (1 if quarter == 3 else 0):at + 4], recv.col.at[quarter])
        prep_cols(ref, quarter)

    def got_rows(step):
        at = GROUPS * step
        landed(ref.rowbuf.at[at:at + (2 if step == 2 else 3)], recv.row.at[step])
        sib_copy(step).start()

    def got_sib(step):
        at = GROUPS * step
        landed(ref.rowbuf.at[at + 3:at + 6], recv.sib.at[step])
        prep_rows(ref, step)

    got_rows(2)
    got_cols(3)
    got_sib(2)
    pair_step(ref, 2, 3)
    got_cols(0)
    pair_step(ref, 2, 0)
    landed(ref.t1.at[1:NROW], recv.t1.at[0])
    lane3 = lax.broadcasted_iota(jnp.int32, (NROW, 1, 128), 2)
    slot3 = lax.broadcasted_iota(jnp.int32, (NROW, 1, 128), 0)
    ref.tvec[...] = jnp.sum(jnp.where(lane3 == slot3, ref.t1[...], 0.0), axis=0)
    for t in range(1, CHUNKS - 1):
        for b in range(2):
            t2_copy(t, b).start()
    got_rows(1)
    got_cols(2)
    got_rows(0)
    pair_step(ref, 2, 2)
    got_sib(1)
    pair_step(ref, 1, 3)
    pair_step(ref, 1, 0)
    pair_step(ref, 1, 2)
    got_cols(1)
    pair_step(ref, 2, 1)
    pair_step(ref, 1, 1)
    got_sib(0)
    for quarter in range(QUART):
        pair_step(ref, 0, quarter)
    landed(ref.t2, recv.t2.at[0])
    pair_weights(ref, town, row)

    lane = lanes()
    own32 = ref.own[...].astype(F32)
    kept_diag = jnp.where((row // 2).astype(F32) < jnp.full((1, 128), town, F32), 1.0, 0.0)
    part = jnp.zeros((1, NROW * M), F32)
    for step in range(SUPER):
        part = part + jnp.sum(ref.usum[step, 0:GROUPS] * ref.wtab[step, 0:GROUPS], axis=0, keepdims=True)
    s2 = jnp.sum(jnp.where(lane < 64, 1.0 / 64, own32 * own32), axis=0, keepdims=True)
    loss = jnp.sum(part, axis=1, keepdims=True) - jnp.sum(s2 * kept_diag, axis=1, keepdims=True)
    count = tfull * (128.0 * 2048.0) - 64.0 * kept_diag
    lossv = jnp.where(lane == 0, loss, jnp.where(lane == 1, count, 0.0))
    ref.lossv[...] = lossv
    ref.la[0] = lossv
    each(1, NCOL, lambda d: la_copy(d).start())

    def cols_out(quarter):
        col_results(ref, quarter)
        for dx in (2, 1, 3, 0):
            if (quarter, dx) != (3, 0):
                rc_copy(quarter, dx).start()

    def rows_out(step):
        row_results(ref, step)
        sg_copy(step).start()

    def rows_on(step):
        landed(ref.sibrecv.at[step], recv.sg.at[step])
        both = ref.rowg[step] + ref.sibrecv[step].astype(F32)
        if step == SUPER - 1:
            ref.rsend[6:8] = both[0:2].astype(BF16)
            ref.rowown[...] = both[2]
        else:
            ref.rsend[3 * step:3 * step + 3] = both.astype(BF16)
        for t in range(3 * step, min(3 * step + 3, CHUNKS - 1)):
            rr_copy(t).start()

    rows_out(0)
    cols_out(1)
    rows_on(0)
    rows_out(1)
    cols_out(0)
    rows_on(1)
    cols_out(2)
    rows_out(2)
    cols_out(3)
    rows_on(2)

    landed(ref.la.at[1:NCOL], recv.la.at[0])
    lsum = jnp.sum(ref.la[...], axis=0)
    ref.lsum[...] = lsum
    ref.lb[0] = lsum
    each(1, NROW, lambda d: lb_copy(d).start())

    total = ref.rowown[...] + ref.colown[...] - jnp.where(lane < 64, 0.0, 2.0 * kept_diag * own32)
    landed(ref.rrow, recv.rr.at[0])
    total = total + jnp.sum(ref.rrow[...].astype(F32), axis=0)
    landed(ref.rcol, recv.rc.at[0])
    total = total + jnp.sum(ref.rcol[...].astype(F32), axis=0)

    landed(ref.lb.at[1:NROW], recv.lb.at[0])
    sums = jnp.sum(ref.lb[...], axis=0)
    pairs = sums[:, 1:2]
    out_loss[...] = sums[:, 0:1] / pairs
    total = total * (EVERYONE / pairs)
    out_x[...] = total[:, :64]
    out_s[...] = total[:, 64:]

    left(ref.t1.at[1:NROW], send.t1.at[0])
    left(ref.t2, send.t2.at[0])
    left(ref.colbuf.at[1:NROW], send.col.at[0])
    left(ref.rrow, send.row.at[0])
    left(ref.rowbuf.at[0:CHUNKS], send.sib.at[0])
    left(ref.sibsend, send.sg.at[0])
    left(ref.rrow, send.rr.at[0])
    left(ref.rcol, send.rc.at[0])
    left(ref.la.at[1:NCOL], send.la.at[0])
    left(ref.lb.at[1:NROW], send.lb.at[0])


def shards(samples, scores, tile_groups):
    vmem = pl.BlockSpec(memory_space=pltpu.VMEM)
    hbm = pl.BlockSpec(memory_space=pl.ANY)
    out_x, out_s, loss = pl.pallas_call(
        kernel,
        out_shape=(
            jax.ShapeDtypeStruct((M, 64), F32),
            jax.ShapeDtypeStruct((M, 64), F32),
            jax.ShapeDtypeStruct((1, 1), F32),
        ),
        in_specs=[hbm, hbm, pl.BlockSpec(memory_space=pltpu.SMEM)],
        out_specs=(vmem, vmem, vmem),
        scratch_shapes=list(SCRATCH.values())
        + [pltpu.SemaphoreType.DMA((n,)) for n in (*SEND.values(), *RECV.values())],
        compiler_params=pltpu.CompilerParams(
            collective_id=0, has_side_effects=True, vmem_limit_bytes=48 * 2**20
        ),
    )(samples, scores, tile_groups)
    return out_x, out_s, loss[0, 0]


def solution(mesh):
    placed = (P(("row", "col"), None), P(("row", "col"), None), P("row", "col"))
    return jax.shard_map(
        shards,
        mesh=mesh,
        in_specs=placed,
        out_specs=(P(("row", "col"), None), P(("row", "col"), None), P()),
        check_vma=False,
    )
```

time: 61 us -> 51.4 us (0.84)
  Pallas kernels: 55 us -> 45.4 us
    pallas_call x1, Pallas kernels: 55 us -> 45.4 us  [shards(): pl.pallas_call(kernel, out_shape=(jax.ShapeDtypeStruct((M, 64), F32), jax...]
where the time goes in v2:
time: 51.4 us; the launch traced here: 51.1 us
  Pallas kernels  45.4 us (88%)
  between operations  3.06 us (6%)
  local copies, waits for them, and re-layouts  2.66 us (5%)
    pallas_call x1, Pallas kernels, shards(): pl.pallas_call(kernel, out_shape=(jax.ShapeDtypeStruct((M, 64), F32), jax...  45.4 us
    unnamed x6, local copies, waits for them, and re-layouts  2.66 us

profile of v2, /device:TPU:1, one launch (start us, length us, event | category | flops | bytes accessed | tf_op | source)
XLA Modules:
  0.0 51.1 jit_solution(902676129714267969)
XLA Ops:
  1.3 0.0 copy-start
  1.3 0.7 %copy-done = bf16[64,64]{1,0:T(8,128)(2,1)S(1)} copy-done((bf16[64,64]{1,0:T(8,128)(2,1)S(1)}, bf16[64,64]{1,0:T(8,128)(2,1)}, u32[]{:S(2)}) %copy-start) | copy-done | bytes 8216
  2.0 0.0 copy-start.1
  2.0 0.7 %copy-done.1 = bf16[64,64]{1,0:T(8,128)(2,1)S(1)} copy-done((bf16[64,64]{1,0:T(8,128)(2,1)S(1)}, bf16[64,64]{1,0:T(8,128)(2,1)}, u32[]{:S(2)}) %copy-start.1) | copy-done | bytes 8216
  2.7 45.4 %shard_map.58 = (f32[64,64]{1,0:T(8,128)S(1)}, f32[64,64]{1,0:T(8,128)S(1)}, f32[1,1]{1,0:T(1,128)}) custom-call(bf16[64,64]{1,0:T(8,128)(2,1)S(1)} %copy-done, bf16[64,64]{1,0:T(8,128)(2,1)S(1)} %copy-done.1, s32[1,1]{1,0:T(1,128)S(6)} %copy.9.groups), custom_call_target="tpu_custom_call" | custom-call | tf_op jit(solution)/shard_map/pallas_call | solution.py:484
  48.1 0.6 %copy.10 = f32[64,64]{1,0:T(8,128)} copy(f32[64,64]{1,0:T(8,128)S(1)} %get-tuple-element.12) | data formatting | bytes 32768
  48.7 0.6 %copy.11 = f32[64,64]{1,0:T(8,128)} copy(f32[64,64]{1,0:T(8,128)S(1)} %get-tuple-element.13) | data formatting | bytes 32768
Async XLA Ops:
  1.3 0.7 %copy-start = (bf16[64,64]{1,0:T(8,128)(2,1)S(1)}, bf16[64,64]{1,0:T(8,128)(2,1)}, u32[]{:S(2)}) copy-start(bf16[64,64]{1,0:T(8,128)(2,1)} %samples.1) | copy-start | bytes 24580
  2.0 0.7 %copy-start.1 = (bf16[64,64]{1,0:T(8,128)(2,1)S(1)}, bf16[64,64]{1,0:T(8,128)(2,1)}, u32[]{:S(2)}) copy-start(bf16[64,64]{1,0:T(8,128)(2,1)} %scores.1) | copy-start | bytes 24580

commit v3 on v2

--- a/solution.py
+++ b/solution.py
@@ -19,6 +19,8 @@
 QUART = 4
 QCOLS = 4 * M
 EVERYONE = float(M * NROW * NCOL)
+FAR_ROW = (10, 8, 9, 11, 6, 14, 4, 12, 5, 7, 13, 15, 2, 1, 3)
+FAR_COL = tuple(sorted(range(1, 32), key=lambda d: -min((d // 2) % 8, 8 - (d // 2) % 8)))
 NSLOT = 14
 
 OFFSETS = (
@@ -249,11 +251,11 @@
     la=pltpu.VMEM((NCOL, 1, 128), F32),
     lb=pltpu.VMEM((NROW, 1, 128), F32),
 )
-SEND = dict(load=2, t1=1, t2=1, col=1, row=1, sib=1, sg=1, rr=1, rc=1, la=1, lb=1)
-RECV = dict(t1=1, t2=1, col=QUART, row=SUPER, sib=SUPER, sg=SUPER, rr=1, rc=1, la=1, lb=1)
-
-
-def kernel(samples, scores, groups, out_x, out_s, out_loss, *rest):
+SEND = dict(load=2, t1=1, t2=1, z=1, col=1, row=1, sib=1, sg=1, rr=1, rc=1, la=1, lb=1)
+RECV = dict(t1=1, t2=1, z=3, col=QUART, row=SUPER, sib=SUPER, sg=SUPER, rr=1, rc=1, la=1, lb=1)
+
+
+def kernel(samples, scores, groups, out, *rest):
     ref = Refs(SCRATCH, rest[:len(SCRATCH)])
     sems = rest[len(SCRATCH):]
     send = Refs(SEND, sems[:len(SEND)])
@@ -263,19 +265,18 @@
     zl, y, core = col // 16, lax.rem(col // 2, 8), lax.rem(col, 2)
     sib = col + 1 - 2 * core
 
-    def each(start, stop, act):
-        def body(d, carry):
-            act(d)
-            return carry
-        lax.fori_loop(start, stop, body, 0)
+    def wrap(value, size):
+        return jnp.where(value >= size, value - size, value)
 
     barrier = pltpu.get_barrier_semaphore()
 
     def greet(to_row, to_col):
         pl.semaphore_signal(barrier, inc=1, device_id=(to_row, to_col), device_id_type=MESH)
 
-    each(1, NROW, lambda d: greet(lax.rem(row + d, NROW), col))
-    each(1, NCOL, lambda d: greet(row, lax.rem(col + d, NCOL)))
+    for d in FAR_ROW:
+        greet(wrap(row + d, NROW), col)
+    for d in FAR_COL:
+        greet(row, wrap(col + d, NCOL))
 
     loads = [pltpu.make_async_copy(samples, ref.xin, send.load.at[0]),
              pltpu.make_async_copy(scores, ref.sin, send.load.at[1])]
@@ -301,17 +302,21 @@
         )
 
     def t1_copy(d):
-        return copy(ref.tsrc, ref.t1.at[NROW - d], send.t1.at[0], recv.t1.at[0], lax.rem(row + d, NROW), col)
+        return copy(ref.tsrc, ref.t1.at[NROW - d], send.t1.at[0], recv.t1.at[0], wrap(row + d, NROW), col)
 
     def t2_copy(t, b):
         chip = chip_at(zl, y, OFFSETS[t], -1)
         slot = 2 * (t - 1) + lax.rem(core + b, 2)
         return copy(ref.tvec, ref.t2.at[slot], send.t2.at[0], recv.t2.at[0], row, 2 * chip + b)
 
+    def z_copy(quarter):
+        to = wrap(zh + 3 - quarter, 4) * 4 + x
+        return copy(ref.own, ref.colbuf.at[quarter * 4], send.z.at[0], recv.z.at[quarter], to, col)
+
     def col_copy(quarter, dx):
-        dz = (quarter + 1) % 4
-        to = lax.rem(zh + 4 - dz, 4) * 4 + lax.rem(x + 4 - dx, 4)
-        return copy(ref.own, ref.colbuf.at[quarter * 4 + dx], send.col.at[0], recv.col.at[quarter], to, col)
+        to = zh * 4 + wrap(x + 4 - dx, 4)
+        src = ref.own if quarter == 3 else ref.colbuf.at[quarter * 4]
+        return copy(src, ref.colbuf.at[quarter * 4 + dx], send.col.at[0], recv.col.at[quarter], to, col)
 
     def row_copy(t):
         chip = chip_at(zl, y, OFFSETS[t], -1)
@@ -331,15 +336,15 @@
 
     def rc_copy(quarter, dx):
         dz = (quarter + 1) % 4
-        to = lax.rem(zh + dz, 4) * 4 + lax.rem(x + dx, 4)
+        to = wrap(zh + dz, 4) * 4 + wrap(x + dx, 4)
         slot = quarter * 4 + dx - (1 if quarter == 3 else 0)
         return copy(ref.csend.at[quarter * 4 + dx], ref.rcol.at[slot], send.rc.at[0], recv.rc.at[0], to, col)
 
     def la_copy(d):
-        return copy(ref.lossv, ref.la.at[NCOL - d], send.la.at[0], recv.la.at[0], row, lax.rem(col + d, NCOL))
+        return copy(ref.lossv, ref.la.at[NCOL - d], send.la.at[0], recv.la.at[0], row, wrap(col + d, NCOL))
 
     def lb_copy(d):
-        return copy(ref.lsum, ref.lb.at[NROW - d], send.lb.at[0], recv.lb.at[0], lax.rem(row + d, NROW), col)
+        return copy(ref.lsum, ref.lb.at[NROW - d], send.lb.at[0], recv.lb.at[0], wrap(row + d, NROW), col)
 
     def landed(buf, sem):
         copy(buf, buf, sem, sem, row, sib).wait_recv()
@@ -347,17 +352,23 @@
     def left(buf, sem):
         copy(buf, buf, sem, sem, row, sib).wait_send()
 
-    each(1, NROW, lambda d: t1_copy(d).start())
+    for d in FAR_ROW:
+        t1_copy(d).start()
+    for quarter in (1, 0, 2):
+        z_copy(quarter).start()
     for t in range(CHUNKS - 1):
         row_copy(t).start()
-    for quarter in (1, 0, 2, 3):
-        for dx in (2, 1, 3, 0):
-            if (quarter, dx) != (3, 0):
-                col_copy(quarter, dx).start()
+    for dx in (2, 1, 3):
+        col_copy(3, dx).start()
+
+    def got_z(quarter):
+        landed(ref.colbuf.at[quarter * 4], recv.z.at[quarter])
+        for dx in (2, 1, 3):
+            col_copy(quarter, dx).start()
 
     def got_cols(quarter):
         at = quarter * 4
-        landed(ref.colbuf.at[at + (1 if quarter == 3 else 0):at + 4], recv.col.at[quarter])
+        landed(ref.colbuf.at[at + 1:at + 4], recv.col.at[quarter])
         prep_cols(ref, quarter)
 
     def got_rows(step):
@@ -370,12 +381,10 @@
         landed(ref.rowbuf.at[at + 3:at + 6], recv.sib.at[step])
         prep_rows(ref, step)
 
+    got_z(0)
+    got_z(2)
     got_rows(2)
-    got_cols(3)
-    got_sib(2)
-    pair_step(ref, 2, 3)
-    got_cols(0)
-    pair_step(ref, 2, 0)
+    got_z(1)
     landed(ref.t1.at[1:NROW], recv.t1.at[0])
     lane3 = lax.broadcasted_iota(jnp.int32, (NROW, 1, 128), 2)
     slot3 = lax.broadcasted_iota(jnp.int32, (NROW, 1, 128), 0)
@@ -384,21 +393,27 @@
         for b in range(2):
             t2_copy(t, b).start()
     got_rows(1)
-    got_cols(2)
     got_rows(0)
-    pair_step(ref, 2, 2)
+    got_cols(3)
+    got_sib(2)
+    pair_step(ref, 2, 3)
+    got_cols(0)
+    pair_step(ref, 2, 0)
     got_sib(1)
     pair_step(ref, 1, 3)
     pair_step(ref, 1, 0)
+    got_cols(2)
+    pair_step(ref, 2, 2)
     pair_step(ref, 1, 2)
-    got_cols(1)
-    pair_step(ref, 2, 1)
-    pair_step(ref, 1, 1)
     got_sib(0)
-    for quarter in range(QUART):
-        pair_step(ref, 0, quarter)
+    pair_step(ref, 0, 3)
+    pair_step(ref, 0, 0)
+    pair_step(ref, 0, 2)
     landed(ref.t2, recv.t2.at[0])
     pair_weights(ref, town, row)
+    got_cols(1)
+    for step in range(SUPER):
+        pair_step(ref, step, 1)
 
     lane = lanes()
     own32 = ref.own[...].astype(F32)
@@ -412,7 +427,8 @@
     lossv = jnp.where(lane == 0, loss, jnp.where(lane == 1, count, 0.0))
     ref.lossv[...] = lossv
     ref.la[0] = lossv
-    each(1, NCOL, lambda d: la_copy(d).start())
+    for d in FAR_COL:
+        la_copy(d).start()
 
     def cols_out(quarter):
         col_results(ref, quarter)
@@ -442,15 +458,15 @@
     cols_out(0)
     rows_on(1)
     cols_out(2)
-    rows_out(2)
-    cols_out(3)
-    rows_on(2)
-
     landed(ref.la.at[1:NCOL], recv.la.at[0])
     lsum = jnp.sum(ref.la[...], axis=0)
     ref.lsum[...] = lsum
     ref.lb[0] = lsum
-    each(1, NROW, lambda d: lb_copy(d).start())
+    for d in FAR_ROW:
+        lb_copy(d).start()
+    rows_out(2)
+    cols_out(3)
+    rows_on(2)
 
     total = ref.rowown[...] + ref.colown[...] - jnp.where(lane < 64, 0.0, 2.0 * kept_diag * own32)
     landed(ref.rrow, recv.rr.at[0])
@@ -461,14 +477,13 @@
     landed(ref.lb.at[1:NROW], recv.lb.at[0])
     sums = jnp.sum(ref.lb[...], axis=0)
     pairs = sums[:, 1:2]
-    out_loss[...] = sums[:, 0:1] / pairs
-    total = total * (EVERYONE / pairs)
-    out_x[...] = total[:, :64]
-    out_s[...] = total[:, 64:]
+    out[0:64, :] = total * (EVERYONE / pairs)
+    out[64:72, :] = jnp.broadcast_to(sums[:, 0:1] / pairs, (8, 128))
 
     left(ref.t1.at[1:NROW], send.t1.at[0])
     left(ref.t2, send.t2.at[0])
-    left(ref.colbuf.at[1:NROW], send.col.at[0])
+    left(ref.colbuf.at[0:3], send.z.at[0])
+    left(ref.colbuf.at[0:12], send.col.at[0])
     left(ref.rrow, send.row.at[0])
     left(ref.rowbuf.at[0:CHUNKS], send.sib.at[0])
     left(ref.sibsend, send.sg.at[0])
@@ -480,22 +495,34 @@
 
 def shards(samples, scores, tile_groups):
     vmem = pl.BlockSpec(memory_space=pltpu.VMEM)
-    hbm = pl.BlockSpec(memory_space=pl.ANY)
+    hbm = pl.BlockSpec(memory_space=pltpu.HBM)
+    out = pl.pallas_call(
+        kernel,
+        out_shape=jax.ShapeDtypeStruct((M + 8, 128), F32),
+        in_specs=[hbm, hbm, pl.BlockSpec(memory_space=pltpu.SMEM)],
+        out_specs=vmem,
+        scratch_shapes=list(SCRATCH.values())
+        + [pltpu.SemaphoreType.DMA((n,)) for n in (*SEND.values(), *RECV.values())],
+        compiler_params=pltpu.CompilerParams(
+            collective_id=0, has_side_effects=True, vmem_limit_bytes=64 * 2**20
+        ),
+    )(samples, scores, tile_groups)
+    def split(whole, out_x, out_s, out_loss):
+        out_x[...] = whole[0:M, 0:64]
+        out_s[...] = whole[0:M, 64:128]
+        out_loss[...] = whole[M:M + 1, 0:1]
+
     out_x, out_s, loss = pl.pallas_call(
-        kernel,
+        split,
         out_shape=(
             jax.ShapeDtypeStruct((M, 64), F32),
             jax.ShapeDtypeStruct((M, 64), F32),
             jax.ShapeDtypeStruct((1, 1), F32),
         ),
-        in_specs=[hbm, hbm, pl.BlockSpec(memory_space=pltpu.SMEM)],
+        in_specs=[vmem],
         out_specs=(vmem, vmem, vmem),
-        scratch_shapes=list(SCRATCH.values())
-        + [pltpu.SemaphoreType.DMA((n,)) for n in (*SEND.values(), *RECV.values())],
-        compiler_params=pltpu.CompilerParams(
-            collective_id=0, has_side_effects=True, vmem_limit_bytes=48 * 2**20
-        ),
-    )(samples, scores, tile_groups)
+        compiler_params=pltpu.CompilerParams(vmem_limit_bytes=64 * 2**20),
+    )(out)
     return out_x, out_s, loss[0, 0]
 
 

time: 51.4 us -> 45.4 us (0.88)
  local copies, waits for them, and re-layouts: 2.66 us -> 0 us
  between operations: 3.06 us -> 1.28 us
  Pallas kernels: 45.4 us -> 43.9 us
    unnamed x6 -> x0, local copies, waits for them, and re-layouts: 2.66 us -> none
    pallas_call x1 -> x2, Pallas kernels: 45.4 us -> 43.9 us  [the longest x1 42.4 us: shards(): pl.pallas_call(kernel, out_shape=jax.ShapeDtypeStruct((M + 8, 128), F32),...]
where the time goes in v3:
time: 45.4 us; the launch traced here: 45.1 us
  Pallas kernels  43.9 us (97%)
  between operations  1.28 us (3%)
    pallas_call x1, Pallas kernels, shards(): pl.pallas_call(kernel, out_shape=jax.ShapeDtypeStruct((M + 8, 128), F32),...  42.4 us
    pallas_call x1, Pallas kernels, shards(): pl.pallas_call(split, out_shape=(jax.ShapeDtypeStruct((M, 64), F32), jax....  1.46 us

profile of v3, /device:TPU:1, one launch (start us, length us, event | category | flops | bytes accessed | tf_op | source)
XLA Modules:
  0.0 45.1 jit_solution(2990160096708447485)
XLA Ops:
  1.3 42.4 %shard_map.58.whole = f32[72,128]{1,0:T(8,128)} custom-call(bf16[64,64]{1,0:T(8,128)(2,1)} %samples.1, bf16[64,64]{1,0:T(8,128)(2,1)} %scores.1, s32[1,1]{1,0:T(1,128)S(6)} %copy.6.groups), custom_call_target="tpu_custom_call" | custom-call | tf_op jit(solution)/shard_map/pallas_call | solution.py:499
  43.7 1.5 %shard_map.59 = (f32[64,64]{1,0:T(8,128)}, f32[64,64]{1,0:T(8,128)}, f32[1,1]{1,0:T(1,128)}) custom-call(f32[72,128]{1,0:T(8,128)} %shard_map.58.whole), custom_call_target="tpu_custom_call" | custom-call | tf_op jit(solution)/shard_map/pallas_call | solution.py:515

commit v4 on v3

--- a/solution.py
+++ b/solution.py
@@ -195,8 +195,7 @@
     gs = g1[64:128] + g1[128:192] + xt * ks
     grad = jnp.concatenate([gx, gs], axis=0).T.reshape(4, M, 128)
     ref.csend[quarter * 4:quarter * 4 + 4] = grad.astype(BF16)
-    if quarter == 3:
-        ref.colown[...] = grad[0]
+    ref.colown[quarter] = grad[0]
 
 
 def chip_at(zl, y, offset, sign):
@@ -243,16 +242,18 @@
     rsend=pltpu.VMEM((CHUNKS - 1, M, 128), BF16),
     csend=pltpu.VMEM((NROW, M, 128), BF16),
     rowown=pltpu.VMEM((M, 128), F32),
-    colown=pltpu.VMEM((M, 128), F32),
+    colown=pltpu.VMEM((QUART, M, 128), F32),
+    xrecv=pltpu.VMEM((2, 3, M, 128), BF16),
+    zsend=pltpu.VMEM((2, M, 128), BF16),
     rrow=pltpu.VMEM((CHUNKS - 1, M, 128), BF16),
-    rcol=pltpu.VMEM((NROW - 1, M, 128), BF16),
+    rcol=pltpu.VMEM((9, M, 128), BF16),
     lossv=pltpu.VMEM((1, 128), F32),
     lsum=pltpu.VMEM((1, 128), F32),
     la=pltpu.VMEM((NCOL, 1, 128), F32),
     lb=pltpu.VMEM((NROW, 1, 128), F32),
 )
-SEND = dict(load=2, t1=1, t2=1, z=1, col=1, row=1, sib=1, sg=1, rr=1, rc=1, la=1, lb=1)
-RECV = dict(t1=1, t2=1, z=3, col=QUART, row=SUPER, sib=SUPER, sg=SUPER, rr=1, rc=1, la=1, lb=1)
+SEND = dict(load=2, t1=1, t2=1, z=1, col=1, row=1, sib=1, sg=1, rr=1, rc=1, xs=1, la=1, lb=1)
+RECV = dict(t1=1, t2=1, z=3, col=QUART, row=SUPER, sib=SUPER, sg=SUPER, rr=1, rc=1, xs=2, la=1, lb=1)
 
 
 def kernel(samples, scores, groups, out, *rest):
@@ -335,10 +336,18 @@
         return copy(ref.rsend.at[t], ref.rrow.at[t], send.rr.at[0], recv.rr.at[0], row, 2 * chip + core)
 
     def rc_copy(quarter, dx):
-        dz = (quarter + 1) % 4
-        to = wrap(zh + dz, 4) * 4 + wrap(x + dx, 4)
-        slot = quarter * 4 + dx - (1 if quarter == 3 else 0)
-        return copy(ref.csend.at[quarter * 4 + dx], ref.rcol.at[slot], send.rc.at[0], recv.rc.at[0], to, col)
+        src = ref.csend.at[quarter * 4 + dx]
+        to_x = wrap(x + dx, 4)
+        if quarter == 1:
+            return copy(src, ref.rcol.at[dx], send.rc.at[0], recv.rc.at[0], wrap(zh + 2, 4) * 4 + to_x, col)
+        if quarter == 3:
+            return copy(src, ref.rcol.at[3 + dx], send.rc.at[0], recv.rc.at[0], zh * 4 + to_x, col)
+        half = quarter // 2
+        return copy(src, ref.xrecv.at[half, dx - 1], send.xs.at[0], recv.xs.at[half], zh * 4 + to_x, col)
+
+    def zs_copy(quarter):
+        to = wrap(zh + quarter + 1, 4) * 4 + x
+        return copy(ref.zsend.at[quarter // 2], ref.rcol.at[7 + quarter // 2], send.rc.at[0], recv.rc.at[0], to, col)
 
     def la_copy(d):
         return copy(ref.lossv, ref.la.at[NCOL - d], send.la.at[0], recv.la.at[0], row, wrap(col + d, NCOL))
@@ -433,8 +442,15 @@
     def cols_out(quarter):
         col_results(ref, quarter)
         for dx in (2, 1, 3, 0):
-            if (quarter, dx) != (3, 0):
+            if quarter == 1 or dx:
                 rc_copy(quarter, dx).start()
+
+    def cols_on(quarter):
+        half = quarter // 2
+        landed(ref.xrecv.at[half], recv.xs.at[half])
+        both = ref.colown[quarter] + jnp.sum(ref.xrecv[half].astype(F32), axis=0)
+        ref.zsend[half] = both.astype(BF16)
+        zs_copy(quarter).start()
 
     def rows_out(step):
         row_results(ref, step)
@@ -453,22 +469,24 @@
 
     rows_out(0)
     cols_out(1)
+    cols_out(0)
+    cols_out(2)
     rows_on(0)
     rows_out(1)
-    cols_out(0)
+    cols_out(3)
     rows_on(1)
-    cols_out(2)
+    rows_out(2)
+    rows_on(2)
     landed(ref.la.at[1:NCOL], recv.la.at[0])
     lsum = jnp.sum(ref.la[...], axis=0)
     ref.lsum[...] = lsum
     ref.lb[0] = lsum
     for d in FAR_ROW:
         lb_copy(d).start()
-    rows_out(2)
-    cols_out(3)
-    rows_on(2)
-
-    total = ref.rowown[...] + ref.colown[...] - jnp.where(lane < 64, 0.0, 2.0 * kept_diag * own32)
+    cols_on(0)
+    cols_on(2)
+
+    total = ref.rowown[...] + ref.colown[3] - jnp.where(lane < 64, 0.0, 2.0 * kept_diag * own32)
     landed(ref.rrow, recv.rr.at[0])
     total = total + jnp.sum(ref.rrow[...].astype(F32), axis=0)
     landed(ref.rcol, recv.rc.at[0])
@@ -489,6 +507,7 @@
     left(ref.sibsend, send.sg.at[0])
     left(ref.rrow, send.rr.at[0])
     left(ref.rcol, send.rc.at[0])
+    left(ref.xrecv, send.xs.at[0])
     left(ref.la.at[1:NCOL], send.la.at[0])
     left(ref.lb.at[1:NROW], send.lb.at[0])
 

time: 45.4 us -> 44.1 us (0.971)
  Pallas kernels: 43.9 us -> 42.5 us
    pallas_call x1, Pallas kernels: 42.4 us -> 41 us  [shards(): pl.pallas_call(kernel, out_shape=jax.ShapeDtypeStruct((M + 8, 128), F32),...]
where the time goes in v4:
time: 44.1 us; the launch traced here: 43.8 us
  Pallas kernels  42.5 us (96%)
  between operations  1.28 us (3%)
    pallas_call x1, Pallas kernels, shards(): pl.pallas_call(kernel, out_shape=jax.ShapeDtypeStruct((M + 8, 128), F32),...  41 us
    pallas_call x1, Pallas kernels, shards(): pl.pallas_call(split, out_shape=(jax.ShapeDtypeStruct((M, 64), F32), jax....  1.46 us

profile of v4, /device:TPU:1, one launch (start us, length us, event | category | flops | bytes accessed | tf_op | source)
XLA Modules:
  0.0 43.8 jit_solution(3342854720325815216)
XLA Ops:
  1.3 41.0 %shard_map.58.whole = f32[72,128]{1,0:T(8,128)} custom-call(bf16[64,64]{1,0:T(8,128)(2,1)} %samples.1, bf16[64,64]{1,0:T(8,128)(2,1)} %scores.1, s32[1,1]{1,0:T(1,128)S(6)} %copy.6.groups), custom_call_target="tpu_custom_call" | custom-call | tf_op jit(solution)/shard_map/pallas_call | solution.py:518
  42.3 1.5 %shard_map.59 = (f32[64,64]{1,0:T(8,128)}, f32[64,64]{1,0:T(8,128)}, f32[1,1]{1,0:T(1,128)}) custom-call(f32[72,128]{1,0:T(8,128)} %shard_map.58.whole), custom_call_target="tpu_custom_call" | custom-call | tf_op jit(solution)/shard_map/pallas_call | solution.py:534

commit v5 on v4

--- a/solution.py
+++ b/solution.py
@@ -179,7 +179,7 @@
     grad = low + jnp.where(lanes() < 64, p * (-cs), high) + sw * (ks * (1.0 / 64))
     grad = grad.reshape(GROUPS, M, 128)
     ref.rowg[step] = grad[0:3]
-    ref.sibsend[step] = grad[3:6].astype(BF16)
+    ref.sibsend[step] = grad[3:6]
 
 
 def col_results(ref, quarter):
@@ -237,8 +237,8 @@
     cmat=pltpu.VMEM((RG * M, NROW * M), BF16),
     usum=pltpu.VMEM((SUPER, 8, NROW * M), F32),
     rowg=pltpu.VMEM((SUPER, 3, M, 128), F32),
-    sibsend=pltpu.VMEM((SUPER, 3, M, 128), BF16),
-    sibrecv=pltpu.VMEM((SUPER, 3, M, 128), BF16),
+    sibsend=pltpu.VMEM((SUPER, 3, M, 128), F32),
+    sibrecv=pltpu.VMEM((SUPER, 3, M, 128), F32),
     rsend=pltpu.VMEM((CHUNKS - 1, M, 128), BF16),
     csend=pltpu.VMEM((NROW, M, 128), BF16),
     rowown=pltpu.VMEM((M, 128), F32),
@@ -418,11 +418,11 @@
     pair_step(ref, 0, 3)
     pair_step(ref, 0, 0)
     pair_step(ref, 0, 2)
-    landed(ref.t2, recv.t2.at[0])
-    pair_weights(ref, town, row)
     got_cols(1)
     for step in range(SUPER):
         pair_step(ref, step, 1)
+    landed(ref.t2, recv.t2.at[0])
+    pair_weights(ref, town, row)
 
     lane = lanes()
     own32 = ref.own[...].astype(F32)
@@ -458,7 +458,7 @@
 
     def rows_on(step):
         landed(ref.sibrecv.at[step], recv.sg.at[step])
-        both = ref.rowg[step] + ref.sibrecv[step].astype(F32)
+        both = ref.rowg[step] + ref.sibrecv[step]
         if step == SUPER - 1:
             ref.rsend[6:8] = both[0:2].astype(BF16)
             ref.rowown[...] = both[2]
@@ -468,14 +468,14 @@
             rr_copy(t).start()
 
     rows_out(0)
-    cols_out(1)
     cols_out(0)
     cols_out(2)
+    cols_out(1)
     rows_on(0)
     rows_out(1)
+    rows_out(2)
     cols_out(3)
     rows_on(1)
-    rows_out(2)
     rows_on(2)
     landed(ref.la.at[1:NCOL], recv.la.at[0])
     lsum = jnp.sum(ref.la[...], axis=0)

time: 44.1 us -> 43.2 us (0.980)
  Pallas kernels: 42.5 us -> 41.6 us
    pallas_call x1, Pallas kernels: 41 us -> 40.1 us  [shards(): pl.pallas_call(kernel, out_shape=jax.ShapeDtypeStruct((M + 8, 128), F32),...]
where the time goes in v5:
time: 43.2 us; the launch traced here: 42.9 us
  Pallas kernels  41.6 us (96%)
  between operations  1.28 us (3%)
    pallas_call x1, Pallas kernels, shards(): pl.pallas_call(kernel, out_shape=jax.ShapeDtypeStruct((M + 8, 128), F32),...  40.1 us
    pallas_call x1, Pallas kernels, shards(): pl.pallas_call(split, out_shape=(jax.ShapeDtypeStruct((M, 64), F32), jax....  1.46 us

profile of v5, /device:TPU:1, one launch (start us, length us, event | category | flops | bytes accessed | tf_op | source)
XLA Modules:
  0.0 42.9 jit_solution(11320645498038298971)
XLA Ops:
  1.3 40.1 %shard_map.58.whole = f32[72,128]{1,0:T(8,128)} custom-call(bf16[64,64]{1,0:T(8,128)(2,1)} %samples.1, bf16[64,64]{1,0:T(8,128)(2,1)} %scores.1, s32[1,1]{1,0:T(1,128)S(6)} %copy.6.groups), custom_call_target="tpu_custom_call" | custom-call | tf_op jit(solution)/shard_map/pallas_call | solution.py:518
  41.4 1.5 %shard_map.59 = (f32[64,64]{1,0:T(8,128)}, f32[64,64]{1,0:T(8,128)}, f32[1,1]{1,0:T(1,128)}) custom-call(f32[72,128]{1,0:T(8,128)} %shard_map.58.whole), custom_call_target="tpu_custom_call" | custom-call | tf_op jit(solution)/shard_map/pallas_call | solution.py:534

commit v6 on v5

--- a/solution.py
+++ b/solution.py
@@ -476,13 +476,13 @@
     rows_out(2)
     cols_out(3)
     rows_on(1)
-    rows_on(2)
     landed(ref.la.at[1:NCOL], recv.la.at[0])
     lsum = jnp.sum(ref.la[...], axis=0)
     ref.lsum[...] = lsum
     ref.lb[0] = lsum
     for d in FAR_ROW:
         lb_copy(d).start()
+    rows_on(2)
     cols_on(0)
     cols_on(2)
 

time: 43.2 us -> 42.9 us (level)
  no operation moved by 1% of the time
where the time goes in v6:
time: 42.9 us; the launch traced here: 42.6 us
  Pallas kernels  41.3 us (96%)
  between operations  1.28 us (3%)
    pallas_call x1, Pallas kernels, shards(): pl.pallas_call(kernel, out_shape=jax.ShapeDtypeStruct((M + 8, 128), F32),...  39.8 us
    pallas_call x1, Pallas kernels, shards(): pl.pallas_call(split, out_shape=(jax.ShapeDtypeStruct((M, 64), F32), jax....  1.46 us

profile of v6, /device:TPU:1, one launch (start us, length us, event | category | flops | bytes accessed | tf_op | source)
XLA Modules:
  0.0 42.6 jit_solution(9560989830181618894)
XLA Ops:
  1.3 39.8 %shard_map.58.whole = f32[72,128]{1,0:T(8,128)} custom-call(bf16[64,64]{1,0:T(8,128)(2,1)} %samples.1, bf16[64,64]{1,0:T(8,128)(2,1)} %scores.1, s32[1,1]{1,0:T(1,128)S(6)} %copy.6.groups), custom_call_target="tpu_custom_call" | custom-call | tf_op jit(solution)/shard_map/pallas_call | solution.py:518
  41.1 1.5 %shard_map.59 = (f32[64,64]{1,0:T(8,128)}, f32[64,64]{1,0:T(8,128)}, f32[1,1]{1,0:T(1,128)}) custom-call(f32[72,128]{1,0:T(8,128)} %shard_map.58.whole), custom_call_target="tpu_custom_call" | custom-call | tf_op jit(solution)/shard_map/pallas_call | solution.py:534
